TPU v7x, 512 devices: a whole 4x4x16 slice. The times are simulated.
512 devices in a mesh: tm: 32 (over y, z_hi, core), space: 16 (over x, z_lo).
Axes of the slice: x: 4, y: 4, z: 16 (z_hi: 4, z_lo: 4; z = z_hi * 4 + z_lo), core: 2. Of those that a mesh axis runs over, the one named last changes fastest.
Arguments:
- queries: bfloat16 [65536, 4096], P(('tm', 'space')), may hold values from -8 to 8
- keys: bfloat16 [65536, 4096], P(('tm', 'space')), may hold values from -8 to 8
- values: bfloat16 [65536, 4096], P(('tm', 'space')), may hold values from -6 to 6
- tile_mask: int32 [512, 512], P('tm'), may hold values from 0 to 1, as said below
Outputs:
- attended: bfloat16 [65536, 4096], P(('tm', 'space'))
Inputs may be any that keep to these rules, and one draw needn't show every extreme that they name: `tile_mask`: tile t holds tokens t * 128 to t * 128 + 127, of frame group t // 16 and height band t % 16. Every diagonal entry is 1. A query tile's ones lie in its own frame group or in the two adjacent ones. Each row has at most 15 ones, and some row exactly 15. For each frame group and each adjacent group that exists, the key tiles of the adjacent group that some query tile of the group uses number exactly 8.
All inputs are finite; a program needn't handle non-finite values.
Results may differ from a plain program's by a relative error of at most 0.0049.
Values may be sent and summed in bfloat16 or wider, within the bound.
A program may use at most 64 MiB of HBM per device.

v0:
```python
import math

import jax
import jax.numpy as jnp
from jax import lax
from jax.sharding import PartitionSpec as P

HEAD_DIM = 128
REACH = 4


def shifted(value, axis, steps):
    count = lax.axis_size(axis)
    leading, last = (max(0, -steps), min(count, count - steps))
    return lax.ppermute(value, axis, [(source, source + steps) for source in range(leading, last)])


def choose_slots(pool_hits, slot_limit):
    order_rank = jnp.cumsum(pool_hits, axis=1) - 1
    slot_ids = jnp.arange(pool_hits.shape[1], dtype=jnp.int32)
    wanted = jnp.arange(slot_limit, dtype=jnp.int32)
    matched = (pool_hits[:, :, None] > 0) & (order_rank[:, :, None] == wanted[None, None, :])
    slots = jnp.sum(jnp.where(matched, slot_ids[None, :, None], 0), axis=1)
    usable = wanted[None, :] < jnp.sum(pool_hits, axis=1)[:, None]
    return (slots, usable)


def body(queries, keys, values, tile_mask):
    band_count = lax.axis_size("space")
    group_count = lax.axis_size("tm")
    group_index = lax.axis_index("tm")
    tile_len = queries.shape[0]
    query_all, key_all, value_all = (
        lax.all_to_all(queries, "space", split_axis=1, concat_axis=0, tiled=True),
        lax.all_to_all(keys, "space", split_axis=1, concat_axis=0, tiled=True),
        lax.all_to_all(values, "space", split_axis=1, concat_axis=0, tiled=True),
    )
    local_width = query_all.shape[1]
    local_heads = local_width // HEAD_DIM
    stacked = jnp.stack([key_all, value_all])
    band_ids = jnp.arange(band_count, dtype=jnp.int32)
    own_ids = group_index * band_count + band_ids
    prior_pool = shifted(stacked, "tm", 1)
    later_pool = shifted(stacked, "tm", -1)
    prior_ids = jnp.where(group_index >= 1, own_ids - band_count, -1)
    later_ids = jnp.where(group_index + 1 < group_count, own_ids + band_count, -1)
    pool = jnp.concatenate([stacked, prior_pool, later_pool], axis=1)
    pool_ids = jnp.concatenate([own_ids, prior_ids, later_ids])
    columns = jnp.arange(tile_mask.shape[1], dtype=jnp.int32)
    pool_hits = jnp.sum(
        jnp.where(pool_ids[None, :, None] == columns[None, None, :], tile_mask[:, None, :], 0),
        axis=2,
    )
    slot_limit = min(2 * REACH + 1, band_count) + 2 * min(3, band_count // 2)
    slots, usable = choose_slots(pool_hits, slot_limit)
    pool_keys = pool[0].reshape(-1, tile_len, local_width)
    pool_values = pool[1].reshape(-1, tile_len, local_width)
    block_size = max(1, min(band_count, 512 // tile_len))
    while band_count % block_size:
        block_size -= 1
    block_count = band_count // block_size
    inv_root = 1.0 / math.sqrt(HEAD_DIM)

    def attend(block_item):
        query_block, slot_block, live_block = block_item
        key_rows = jnp.take(pool_keys, slot_block, axis=0).reshape(
            block_size, slot_limit * tile_len, local_heads, HEAD_DIM
        )
        value_rows = jnp.take(pool_values, slot_block, axis=0).reshape(
            block_size, slot_limit * tile_len, local_heads, HEAD_DIM
        )
        key_live = jnp.repeat(live_block, tile_len, axis=1)
        scores = (
            jnp.einsum("bqhd,bkhd->bhqk", query_block, key_rows, preferred_element_type=jnp.float32)
            * inv_root
        )
        scores = jnp.where(key_live[:, None, None, :], scores, -jnp.inf)
        row_top = jnp.max(scores, axis=3, keepdims=True)
        raised = jnp.exp(scores - row_top)
        weights = (raised / jnp.sum(raised, axis=3, keepdims=True)).astype(jnp.bfloat16)
        output = jnp.einsum(
            "bhqk,bkhd->bqhd", weights, value_rows, preferred_element_type=jnp.float32
        )
        return output.astype(jnp.bfloat16)

    query_blocks = query_all.reshape(block_count, block_size, tile_len, local_heads, HEAD_DIM)
    outputs = lax.map(
        attend,
        (
            query_blocks,
            slots.reshape(block_count, block_size, slot_limit),
            usable.reshape(block_count, block_size, slot_limit),
        ),
    )
    attended_local = outputs.reshape(band_count * tile_len, local_width)
    return lax.all_to_all(attended_local, "space", split_axis=0, concat_axis=1, tiled=True)


def solution(mesh):
    placed = (
        P(("tm", "space"), None),
        P(("tm", "space"), None),
        P(("tm", "space"), None),
        P("tm", None),
    )
    return jax.shard_map(
        body, mesh=mesh, in_specs=placed, out_specs=P(("tm", "space"), None), check_vma=False
    )
```

profile of v0, /device:TPU:25, one launch (start us, length us, event | category | flops | bytes accessed | tf_op | source)
XLA Modules:
  0.0 416.3 jit_solution(15220486150948265840)
XLA Ops:
  0.0 1.7 copy.47
  1.7 1.3 copy.48
  3.0 8.2 %all-to-all-start = ((bf16[128,16,256]{2,0,1:T(8,128)(2,1)}), bf16[128,16,256]{2,0,1:T(8,128)(2,1)S(1)}, u32[]{:S(2)}, u32[]{:S(2)}) async-start(bf16[128,16,256]{2,0,1:T(8,128)(2,1)} %copy.48), calls=%async_computation | async-start | bytes 2097152 | tf_op jit(solution)/shard_map/all_to_all | solution.py:35
  11.2 0.7 copy.49
  11.9 0.5 copy.50
  12.4 25.8 %all-to-all-done = bf16[128,16,256]{2,0,1:T(8,128)(2,1)S(1)} async-done(((bf16[128,16,256]{2,0,1:T(8,128)(2,1)}), bf16[128,16,256]{2,0,1:T(8,128)(2,1)S(1)}, u32[]{:S(2)}, u32[]{:S(2)}) %all-to-all-start) | async-done | bytes 1048608 | tf_op jit(solution)/shard_map/all_to_all | solution.py:35
  38.2 31.2 %all_to_all.67 = bf16[128,16,256]{2,0,1:T(8,128)(2,1)S(1)} all-to-all(bf16[128,16,256]{2,0,1:T(8,128)(2,1)S(1)} %copy.50), channel_id=1, replica_groups=mesh['tm'=32,'space'=16] {'space'}, dimensions={1} | all-to-all | bytes 2097152 | tf_op jit(solution)/shard_map/all_to_all | solution.py:36
  69.4 1.5 pad_maximum_fusion.1
  70.9 10.4 %collective-permute-start = (bf16[2,2048,256]{2,1,0:T(8,128)(2,1)}, bf16[2,2048,256]{2,1,0:T(8,128)(2,1)}, u32[]{:S(2)}, u32[]{:S(2)}) collective-permute-start(bf16[2,2048,256]{2,1,0:T(8,128)(2,1)} %pad_maximum_fusion.1), channel_id=1, source_target_pairs={{0,16},{16,32},{32,48},{48,64},{64,80},{80,96},{96,112},{112,128},... | collective-permute-start | bytes 6291464 | tf_op jit(solution)/shard_map/ppermute | solution.py:15
  81.3 1.9 collective-permute-start.1
  83.3 1.3 copy.51
  84.6 4.5 %all-to-all-start.2 = ((bf16[128,16,256]{0,2,1:T(8,128)(2,1)}), bf16[128,16,256]{0,2,1:T(8,128)(2,1)}, u32[]{:S(2)}, u32[]{:S(2)}) async-start(bf16[128,16,256]{0,2,1:T(8,128)(2,1)} %bitcast.15), calls=%async_computation.2 | async-start | bytes 2097152 | tf_op jit(solution)/shard_map/all_to_all | solution.py:34
  89.3 0.1 iota_compare_fusion.1
  89.4 0.7 select_reduce_fusion
  90.0 0.2 reduce_window_sum.11
  90.3 0.4 select_reduce_fusion.2
  90.6 0.1 copy.46
  90.7 0.1 lt.30
  90.9 22.2 %collective-permute-done = bf16[2,2048,256]{2,1,0:T(8,128)(2,1)} collective-permute-done((bf16[2,2048,256]{2,1,0:T(8,128)(2,1)}, bf16[2,2048,256]{2,1,0:T(8,128)(2,1)}, u32[]{:S(2)}, u32[]{:S(2)}) %collective-permute-start) | collective-permute-done | bytes 2097184 | tf_op jit(solution)/shard_map/ppermute | solution.py:15
  113.1 10.6 %collective-permute-done.1 = bf16[2,2048,256]{2,1,0:T(8,128)(2,1)} collective-permute-done((bf16[2,2048,256]{2,1,0:T(8,128)(2,1)}, bf16[2,2048,256]{2,1,0:T(8,128)(2,1)}, u32[]{:S(2)}, u32[]{:S(2)}) %collective-permute-start.1) | collective-permute-done | bytes 2097184 | tf_op jit(solution)/shard_map/ppermute | solution.py:15
  123.7 8.9 %pad_maximum_fusion = bf16[2,6144,256]{2,1,0:T(8,128)(2,1)S(1)} fusion(bf16[2,2048,256]{2,1,0:T(8,128)(2,1)} %collective-permute-done.1, bf16[2,2048,256]{2,1,0:T(8,128)(2,1)} %collective-permute-done, bf16[1,2048,256]{2,1,0:T(8,128)(2,1)S(1)} %bitcast.66, bf16[1,2048,256]{2,1,0:T(8,128)(2,1)S(1)} %bitcast.64), kind=kLoop, calls=%fused_computation.30 | loop fusion | flops 25165824 | bytes 12582912 | tf_op jit(solution)/shard_map/concatenate | solution.py:47
  132.6 2.1 fusion.25
  134.6 42.9 %all-to-all-done.2 = bf16[128,16,256]{0,2,1:T(8,128)(2,1)} async-done(((bf16[128,16,256]{0,2,1:T(8,128)(2,1)}), bf16[128,16,256]{0,2,1:T(8,128)(2,1)}, u32[]{:S(2)}, u32[]{:S(2)}) %all-to-all-start.2) | async-done | bytes 1048608 | tf_op jit(solution)/shard_map/all_to_all | solution.py:34
  177.5 178.9 %while.10 = (s32[]{:T(128)}, bf16[4,4,128,2,128]{2,4,3,1,0:T(8,128)(2,1)}, s32[4,4,15]{2,1,0:T(4,128)S(1)}, bf16[48,128,256]{2,1,0:T(8,128)(2,1)}, pred[4,4,15]{...) while((s32[]{:T(128)}, ...), condition=%wide.region_7.9_spmd, body=%wide.region_4.8_spmd.sunk | while | flops 1026428160 | bytes 87077912 | solution.py:87
  177.5 0.1 reshape.123
  177.6 4.6 %gather_fusion = bf16[60,128,256]{2,1,0:T(8,128)(2,1)} fusion(bf16[48,128,256]{2,1,0:T(8,128)(2,1)} %get-tuple-element.179, s32[1024]{0:T(1024)S(1)} %pad_clamp_fusion.2), kind=kCustom, calls=%fused_computation.clone.clone.1 | custom fusion | bytes 7864560 | tf_op jit(solution)/shard_map/while/body/eval_jaxpr/jit(_take)/gather | solution.py:69
  182.2 2.8 gather_fusion.1
  185.0 5.6 %broadcast_select_fusion.5 = (bf16[4,15,128,256]{3,2,1,0:T(8,128)(2,1)}, bf16[4,15,128,256]{3,2,1,0:T(8,128)(2,1)}) fusion(bf16[4,15,128,256]{3,2,1,0:T(8,128)(2,1)} %bitcast.59, pred[4,15]{1,0:T(4,128)(4,1)S(1)} %get-tuple-element.155, bf16[4,15,128,256]{3,2,1,0:T(8,128)(2,1)} %bitcast.60), kind=kLoop, calls=%fused_computation.14.clone.1 | loop fusion | flops 3932160 | bytes 15728700 | tf_op jit(solution)/shard_map/while/body/eval_jaxpr/jit(_take)/select_n | solution.py:69
  190.6 8.3 %reshape.124 = bf16[4,1920,2,128]{3,2,1,0:T(2,128)(2,1)} reshape(bf16[4,15,128,256]{3,2,1,0:T(8,128)(2,1)} %get-tuple-element.156) | data formatting | bytes 7864320 | tf_op jit(solution)/shard_map/while/body/eval_jaxpr/reshape | solution.py:66
  198.9 3.5 fusion.35
  202.6 4.5 %fusion.36 = (f32[4,2,128]{2,1,0:T(2,128)S(1)}, f32[4,2,128,1920]{3,2,1,0:T(8,128)}) fusion(f32[4,2,128,1920]{3,2,1,0:T(8,128)S(1)} %fusion.35, pred[4,1920]{1,0:T(4,128)(4,1)S(1)} %bitcast.71), kind=kOutput, calls=%fused_computation.45.clone.1 | output fusion | flops 11798399 | bytes 15740416 | tf_op jit(solution)/shard_map/while/body/eval_jaxpr/sub | solution.py:79
  207.0 8.3 %reshape.125 = bf16[4,1920,2,128]{3,2,1,0:T(2,128)(2,1)} reshape(bf16[4,15,128,256]{3,2,1,0:T(8,128)(2,1)} %get-tuple-element.159) | data formatting | bytes 7864320 | tf_op jit(solution)/shard_map/while/body/eval_jaxpr/reshape | solution.py:69
  215.4 6.9 %fusion.37 = bf16[4,4,128,2,128]{2,4,3,1,0:T(8,128)(2,1)} fusion(bf16[4,4,128,2,128]{2,4,3,1,0:T(8,128)(2,1)} %get-tuple-element.169, s32[]{:T(128)} %get-tuple-element.168, f32[4,2,128,1920]{3,2,1,0:T(8,128)} %get-tuple-element.157, f32[4,2,128]{2,1,0:T(2,128)S(1)} %get-tuple-element.158, bf16[4,1920,2,128]{3,2,1,0:T(2,128)(2,1)} %reshape.125), kind=kOutput, calls=%fused_computation.18.clone.1 | convolution fusion | flops 507379712 | bytes 12063232 | tf_op jit(solution)/shard_map/while/body/eval_jaxpr/bhqk,bkhd->bqhd/dot_general | solution.py:81
  222.2 0.1 reshape.123
  222.3 4.6 %gather_fusion = bf16[60,128,256]{2,1,0:T(8,128)(2,1)} fusion(bf16[48,128,256]{2,1,0:T(8,128)(2,1)} %get-tuple-element.179, s32[1024]{0:T(1024)S(1)} %pad_clamp_fusion.2), kind=kCustom, calls=%fused_computation.clone.clone.1 | custom fusion | bytes 7864560 | tf_op jit(solution)/shard_map/while/body/eval_jaxpr/jit(_take)/gather | solution.py:69
  227.0 2.8 gather_fusion.1
  229.7 5.6 %broadcast_select_fusion.5 = (bf16[4,15,128,256]{3,2,1,0:T(8,128)(2,1)}, bf16[4,15,128,256]{3,2,1,0:T(8,128)(2,1)}) fusion(bf16[4,15,128,256]{3,2,1,0:T(8,128)(2,1)} %bitcast.59, pred[4,15]{1,0:T(4,128)(4,1)S(1)} %get-tuple-element.155, bf16[4,15,128,256]{3,2,1,0:T(8,128)(2,1)} %bitcast.60), kind=kLoop, calls=%fused_computation.14.clone.1 | loop fusion | flops 3932160 | bytes 15728700 | tf_op jit(solution)/shard_map/while/body/eval_jaxpr/jit(_take)/select_n | solution.py:69
  235.3 8.3 %reshape.124 = bf16[4,1920,2,128]{3,2,1,0:T(2,128)(2,1)} reshape(bf16[4,15,128,256]{3,2,1,0:T(8,128)(2,1)} %get-tuple-element.156) | data formatting | bytes 7864320 | tf_op jit(solution)/shard_map/while/body/eval_jaxpr/reshape | solution.py:66
  243.7 3.5 fusion.35
  247.3 4.5 %fusion.36 = (f32[4,2,128]{2,1,0:T(2,128)S(1)}, f32[4,2,128,1920]{3,2,1,0:T(8,128)}) fusion(f32[4,2,128,1920]{3,2,1,0:T(8,128)S(1)} %fusion.35, pred[4,1920]{1,0:T(4,128)(4,1)S(1)} %bitcast.71), kind=kOutput, calls=%fused_computation.45.clone.1 | output fusion | flops 11798399 | bytes 15740416 | tf_op jit(solution)/shard_map/while/body/eval_jaxpr/sub | solution.py:79
  251.8 8.3 %reshape.125 = bf16[4,1920,2,128]{3,2,1,0:T(2,128)(2,1)} reshape(bf16[4,15,128,256]{3,2,1,0:T(8,128)(2,1)} %get-tuple-element.159) | data formatting | bytes 7864320 | tf_op jit(solution)/shard_map/while/body/eval_jaxpr/reshape | solution.py:69
  260.1 6.9 %fusion.37 = bf16[4,4,128,2,128]{2,4,3,1,0:T(8,128)(2,1)} fusion(bf16[4,4,128,2,128]{2,4,3,1,0:T(8,128)(2,1)} %get-tuple-element.169, s32[]{:T(128)} %get-tuple-element.168, f32[4,2,128,1920]{3,2,1,0:T(8,128)} %get-tuple-element.157, f32[4,2,128]{2,1,0:T(2,128)S(1)} %get-tuple-element.158, bf16[4,1920,2,128]{3,2,1,0:T(2,128)(2,1)} %reshape.125), kind=kOutput, calls=%fused_computation.18.clone.1 | convolution fusion | flops 507379712 | bytes 12063232 | tf_op jit(solution)/shard_map/while/body/eval_jaxpr/bhqk,bkhd->bqhd/dot_general | solution.py:81
  267.0 0.1 reshape.123
  267.1 4.6 %gather_fusion = bf16[60,128,256]{2,1,0:T(8,128)(2,1)} fusion(bf16[48,128,256]{2,1,0:T(8,128)(2,1)} %get-tuple-element.179, s32[1024]{0:T(1024)S(1)} %pad_clamp_fusion.2), kind=kCustom, calls=%fused_computation.clone.clone.1 | custom fusion | bytes 7864560 | tf_op jit(solution)/shard_map/while/body/eval_jaxpr/jit(_take)/gather | solution.py:69
  271.7 2.8 gather_fusion.1
  274.5 5.6 %broadcast_select_fusion.5 = (bf16[4,15,128,256]{3,2,1,0:T(8,128)(2,1)}, bf16[4,15,128,256]{3,2,1,0:T(8,128)(2,1)}) fusion(bf16[4,15,128,256]{3,2,1,0:T(8,128)(2,1)} %bitcast.59, pred[4,15]{1,0:T(4,128)(4,1)S(1)} %get-tuple-element.155, bf16[4,15,128,256]{3,2,1,0:T(8,128)(2,1)} %bitcast.60), kind=kLoop, calls=%fused_computation.14.clone.1 | loop fusion | flops 3932160 | bytes 15728700 | tf_op jit(solution)/shard_map/while/body/eval_jaxpr/jit(_take)/select_n | solution.py:69
  280.1 8.3 %reshape.124 = bf16[4,1920,2,128]{3,2,1,0:T(2,128)(2,1)} reshape(bf16[4,15,128,256]{3,2,1,0:T(8,128)(2,1)} %get-tuple-element.156) | data formatting | bytes 7864320 | tf_op jit(solution)/shard_map/while/body/eval_jaxpr/reshape | solution.py:66
  288.4 3.5 fusion.35
  292.0 4.5 %fusion.36 = (f32[4,2,128]{2,1,0:T(2,128)S(1)}, f32[4,2,128,1920]{3,2,1,0:T(8,128)}) fusion(f32[4,2,128,1920]{3,2,1,0:T(8,128)S(1)} %fusion.35, pred[4,1920]{1,0:T(4,128)(4,1)S(1)} %bitcast.71), kind=kOutput, calls=%fused_computation.45.clone.1 | output fusion | flops 11798399 | bytes 15740416 | tf_op jit(solution)/shard_map/while/body/eval_jaxpr/sub | solution.py:79
  296.5 8.3 %reshape.125 = bf16[4,1920,2,128]{3,2,1,0:T(2,128)(2,1)} reshape(bf16[4,15,128,256]{3,2,1,0:T(8,128)(2,1)} %get-tuple-element.159) | data formatting | bytes 7864320 | tf_op jit(solution)/shard_map/while/body/eval_jaxpr/reshape | solution.py:69
  304.8 6.9 %fusion.37 = bf16[4,4,128,2,128]{2,4,3,1,0:T(8,128)(2,1)} fusion(bf16[4,4,128,2,128]{2,4,3,1,0:T(8,128)(2,1)} %get-tuple-element.169, s32[]{:T(128)} %get-tuple-element.168, f32[4,2,128,1920]{3,2,1,0:T(8,128)} %get-tuple-element.157, f32[4,2,128]{2,1,0:T(2,128)S(1)} %get-tuple-element.158, bf16[4,1920,2,128]{3,2,1,0:T(2,128)(2,1)} %reshape.125), kind=kOutput, calls=%fused_computation.18.clone.1 | convolution fusion | flops 507379712 | bytes 12063232 | tf_op jit(solution)/shard_map/while/body/eval_jaxpr/bhqk,bkhd->bqhd/dot_general | solution.py:81
  311.7 0.1 reshape.123
  311.8 4.6 %gather_fusion = bf16[60,128,256]{2,1,0:T(8,128)(2,1)} fusion(bf16[48,128,256]{2,1,0:T(8,128)(2,1)} %get-tuple-element.179, s32[1024]{0:T(1024)S(1)} %pad_clamp_fusion.2), kind=kCustom, calls=%fused_computation.clone.clone.1 | custom fusion | bytes 7864560 | tf_op jit(solution)/shard_map/while/body/eval_jaxpr/jit(_take)/gather | solution.py:69
  316.4 2.8 gather_fusion.1
  319.2 5.6 %broadcast_select_fusion.5 = (bf16[4,15,128,256]{3,2,1,0:T(8,128)(2,1)}, bf16[4,15,128,256]{3,2,1,0:T(8,128)(2,1)}) fusion(bf16[4,15,128,256]{3,2,1,0:T(8,128)(2,1)} %bitcast.59, pred[4,15]{1,0:T(4,128)(4,1)S(1)} %get-tuple-element.155, bf16[4,15,128,256]{3,2,1,0:T(8,128)(2,1)} %bitcast.60), kind=kLoop, calls=%fused_computation.14.clone.1 | loop fusion | flops 3932160 | bytes 15728700 | tf_op jit(solution)/shard_map/while/body/eval_jaxpr/jit(_take)/select_n | solution.py:69
  324.8 8.3 %reshape.124 = bf16[4,1920,2,128]{3,2,1,0:T(2,128)(2,1)} reshape(bf16[4,15,128,256]{3,2,1,0:T(8,128)(2,1)} %get-tuple-element.156) | data formatting | bytes 7864320 | tf_op jit(solution)/shard_map/while/body/eval_jaxpr/reshape | solution.py:66
  333.1 3.5 fusion.35
  336.8 4.5 %fusion.36 = (f32[4,2,128]{2,1,0:T(2,128)S(1)}, f32[4,2,128,1920]{3,2,1,0:T(8,128)}) fusion(f32[4,2,128,1920]{3,2,1,0:T(8,128)S(1)} %fusion.35, pred[4,1920]{1,0:T(4,128)(4,1)S(1)} %bitcast.71), kind=kOutput, calls=%fused_computation.45.clone.1 | output fusion | flops 11798399 | bytes 15740416 | tf_op jit(solution)/shard_map/while/body/eval_jaxpr/sub | solution.py:79
  341.2 8.3 %reshape.125 = bf16[4,1920,2,128]{3,2,1,0:T(2,128)(2,1)} reshape(bf16[4,15,128,256]{3,2,1,0:T(8,128)(2,1)} %get-tuple-element.159) | data formatting | bytes 7864320 | tf_op jit(solution)/shard_map/while/body/eval_jaxpr/reshape | solution.py:69
  349.6 6.9 %fusion.37 = bf16[4,4,128,2,128]{2,4,3,1,0:T(8,128)(2,1)} fusion(bf16[4,4,128,2,128]{2,4,3,1,0:T(8,128)(2,1)} %get-tuple-element.169, s32[]{:T(128)} %get-tuple-element.168, f32[4,2,128,1920]{3,2,1,0:T(8,128)} %get-tuple-element.157, f32[4,2,128]{2,1,0:T(2,128)S(1)} %get-tuple-element.158, bf16[4,1920,2,128]{3,2,1,0:T(2,128)(2,1)} %reshape.125), kind=kOutput, calls=%fused_computation.18.clone.1 | convolution fusion | flops 507379712 | bytes 12063232 | tf_op jit(solution)/shard_map/while/body/eval_jaxpr/bhqk,bkhd->bqhd/dot_general | solution.py:81
  356.4 1.5 copy.56
  357.9 56.4 %all_to_all.68 = bf16[16,128,256]{2,1,0:T(8,128)(2,1)S(1)} all-to-all(bf16[16,128,256]{2,1,0:T(8,128)(2,1)S(1)} %copy.56), channel_id=1, replica_groups=mesh['tm'=32,'space'=16] {'space'}, dimensions={0} | all-to-all | bytes 2097152 | tf_op jit(solution)/shard_map/all_to_all | solution.py:96
  414.3 0.7 copy.54
  415.0 1.3 copy.55
  (33 shorter events, 0.6 us)
Async XLA Ops:
  0.0 11.2 %copy-start = (bf16[128,4096]{1,0:T(8,128)(2,1)S(1)}, bf16[128,4096]{1,0:T(8,128)(2,1)}, u32[]{:S(2)}) copy-start(bf16[128,4096]{1,0:T(8,128)(2,1)} %param.10) | copy-start | bytes 3145732
  3.0 35.2 %all-to-all-start = ((bf16[128,16,256]{2,0,1:T(8,128)(2,1)}), bf16[128,16,256]{2,0,1:T(8,128)(2,1)S(1)}, u32[]{:S(2)}, u32[]{:S(2)}) async-start(bf16[128,16,256]{2,0,1:T(8,128)(2,1)} %copy.48), calls=%async_computation | async-start | bytes 2097152 | tf_op jit(solution)/shard_map/all_to_all | solution.py:35
  69.4 13.9 %copy-start.1 = (bf16[128,4096]{1,0:T(8,128)(2,1)S(1)}, bf16[128,4096]{1,0:T(8,128)(2,1)}, u32[]{:S(2)}) copy-start(bf16[128,4096]{1,0:T(8,128)(2,1)} %param.8) | copy-start | bytes 3145732
  69.4 20.0 %copy-start.2 = (s32[16,512]{1,0:T(8,128)S(1)}, s32[16,512]{1,0:T(8,128)}, u32[]{:S(2)}) copy-start(s32[16,512]{1,0:T(8,128)} %param.11) | copy-start | bytes 98308
  70.9 42.2 %collective-permute-start = (bf16[2,2048,256]{2,1,0:T(8,128)(2,1)}, bf16[2,2048,256]{2,1,0:T(8,128)(2,1)}, u32[]{:S(2)}, u32[]{:S(2)}) collective-permute-start(bf16[2,2048,256]{2,1,0:T(8,128)(2,1)} %pad_maximum_fusion.1), channel_id=1, source_target_pairs={{0,16},{16,32},{32,48},{48,64},{64,80},{80,96},{96,112},{112,128},... | collective-permute-start | bytes 6291464 | tf_op jit(solution)/shard_map/ppermute | solution.py:15
  81.3 42.4 %collective-permute-start.1 = (bf16[2,2048,256]{2,1,0:T(8,128)(2,1)}, bf16[2,2048,256]{2,1,0:T(8,128)(2,1)}, u32[]{:S(2)}, u32[]{:S(2)}) collective-permute-start(bf16[2,2048,256]{2,1,0:T(8,128)(2,1)} %pad_maximum_fusion.1), channel_id=1, source_target_pairs={{16,0},{32,16},{48,32},{64,48},{80,64},{96,80},{112,96},{128,112},... | collective-permute-start | bytes 6291464 | tf_op jit(solution)/shard_map/ppermute | solution.py:15
  84.6 92.9 %all-to-all-start.2 = ((bf16[128,16,256]{0,2,1:T(8,128)(2,1)}), bf16[128,16,256]{0,2,1:T(8,128)(2,1)}, u32[]{:S(2)}, u32[]{:S(2)}) async-start(bf16[128,16,256]{0,2,1:T(8,128)(2,1)} %bitcast.15), calls=%async_computation.2 | async-start | bytes 2097152 | tf_op jit(solution)/shard_map/all_to_all | solution.py:34
where the time goes:
time: 418 us; the launch traced here: 416 us
  local copies, waits for them, and re-layouts  108 us (26%)
  waiting for transfers between devices  101 us (24%)
  blocking collectives  87.5 us (21%)
  other arithmetic  52.3 us (13%)
  matrix products  41.5 us (10%)
  starting transfers between devices  25 us (6%)
    all_to_all x1, blocking collectives, body(): lax.all_to_all(attended_local, 'space', split_axis=0, concat_axis=1, tile...  56.4 us
    all_to_all x1, waiting for transfers between devices, body(): lax.all_to_all(queries, 'space', split_axis=1, concat_axis=0, tiled=True)  42.9 us
    reshape x4, local copies, waits for them, and re-layouts, attend(): jnp.take(pool_values, slot_block, axis=0)  33.3 us
    reshape x4, local copies, waits for them, and re-layouts, attend(): jnp.take(pool_keys, slot_block, axis=0)  33.2 us
    ppermute x2, waiting for transfers between devices, shifted(): lax.ppermute(value, axis, [(source, source + steps) for source in range(l...  32.8 us
    all_to_all x1, blocking collectives, body(): lax.all_to_all(values, 'space', split_axis=1, concat_axis=0, tiled=True)  31.2 us
    dot_general x4, matrix products, attend(): jnp.einsum('bhqk,bkhd->bqhd', weights, value_rows, preferred_element_type...  27.5 us
    all_to_all x1, waiting for transfers between devices, body(): lax.all_to_all(keys, 'space', split_axis=1, concat_axis=0, tiled=True)  25.8 us
  transfers between devices with their start and end apart: 4, of which 4 were waited for; matrix products, arithmetic and copies ran while one was open for 4% of the time, Pallas kernels for 0%

commit v1 on v0

v1 whole, which is shorter than its diff:
```python
import functools
import math

import jax
import jax.numpy as jnp
from jax import lax
from jax.experimental import pallas as pl
from jax.experimental.pallas import tpu as pltpu
from jax.sharding import PartitionSpec as P

HEAD_DIM = 128
REACH = 4
UMAX = 8
PICKS = 3
MASKED = -1e30
MESH = pl.DeviceIdType.MESH


def adjacent(tile_mask, group, bands, exists):
    block = lax.dynamic_slice(tile_mask, (0, group * bands), (bands, bands))
    block = jnp.where(exists, block, 0)
    ids = jnp.arange(bands, dtype=jnp.int32)
    upto = (ids[:, None] <= ids[None, :]).astype(jnp.int32)
    used = jnp.max(block, axis=0)
    place = jnp.sum(used[:, None] * upto, axis=0) - 1
    slots = jnp.arange(UMAX, dtype=jnp.int32)
    hit = (used[:, None] > 0) & (place[:, None] == slots[None, :])
    tiles = jnp.sum(jnp.where(hit, ids[:, None], 0), axis=0)
    order = jnp.sum(block[:, :, None] * upto[None], axis=1) - 1
    wanted = jnp.arange(PICKS, dtype=jnp.int32)
    taken = (block[:, :, None] > 0) & (order[:, :, None] == wanted)
    picks = jnp.sum(jnp.where(taken, place[None, :, None], 0), axis=1)
    live = jnp.sum(taken.astype(jnp.int32), axis=1)
    return tiles, picks, live


def kernel(
    bands, groups, heads,
    meta, lists, q_in, k_in, v_in, out,
    *scratch,
):
    q_all, k_all, v_all, o_all = (scratch[i * heads : (i + 1) * heads] for i in range(4))
    halo_out = [scratch[(4 + i) * heads : (5 + i) * heads] for i in range(2)]
    halo_in = [scratch[(6 + i) * heads : (7 + i) * heads] for i in range(2)]
    (own_sem, send_sem, recv_sem, halo_send, halo_recv, o_own, o_send, o_recv) = scratch[8 * heads :]
    g = lax.axis_index("tm")
    me = lax.axis_index("space")
    tile = q_in.shape[0]
    window = min(2 * REACH + 1, bands)

    barrier = pltpu.get_barrier_semaphore()

    @pl.loop(1, bands)
    def _(d):
        pl.semaphore_signal(barrier, inc=1, device_id={"space": lax.rem(me + d, bands)}, device_id_type=MESH)

    for step in (1, groups - 1):
        pl.semaphore_signal(barrier, inc=1, device_id={"tm": lax.rem(g + step, groups)}, device_id_type=MESH)

    def own_copies():
        found = []
        for a, (source, target) in enumerate(((k_in, k_all), (v_in, v_all), (q_in, q_all))):
            for h in range(heads):
                columns = pl.ds(pl.multiple_of((me * heads + h) * HEAD_DIM, HEAD_DIM), HEAD_DIM)
                found.append(pltpu.make_async_copy(source.at[:, columns], target[h].at[me], own_sem.at[a, h]))
        return found

    for copy in own_copies():
        copy.start()

    pl.semaphore_wait(barrier, bands + 1)

    def spread(a, h, peer, source_band):
        source, target = ((k_in, k_all), (v_in, v_all), (q_in, q_all))[a]
        columns = pl.ds(pl.multiple_of((peer * heads + h) * HEAD_DIM, HEAD_DIM), HEAD_DIM)
        return pltpu.make_async_remote_copy(
            src_ref=source.at[:, columns],
            dst_ref=target[h].at[source_band],
            send_sem=send_sem.at[a, h, peer],
            recv_sem=recv_sem.at[a, h, source_band],
            device_id={"space": peer},
            device_id_type=MESH,
        )

    def start_spread(a, h):
        @pl.loop(1, bands)
        def _(d):
            peer = lax.rem(me + d, bands)
            spread(a, h, peer, me).start()

    def wait_spread(a, h):
        @pl.loop(1, bands)
        def _(d):
            peer = lax.rem(me + d, bands)
            spread(a, h, peer, peer).wait_recv()

    for a, h in [(0, 0), (1, 0), (0, 1), (1, 1), (2, 0), (2, 1)][: 3 * heads]:
        start_spread(a, h)
    for copy in own_copies():
        copy.wait()

    def halo(side, h):
        return pltpu.make_async_remote_copy(
            src_ref=halo_out[side][h],
            dst_ref=halo_in[side][h],
            send_sem=halo_send.at[side, h],
            recv_sem=halo_recv.at[side, h],
            device_id={"tm": g + 1 if side == 0 else g - 1},
            device_id_type=MESH,
        )

    sends = (g < groups - 1, g > 0)
    receives = (g > 0, g < groups - 1)

    for h in range(heads):
        wait_spread(0, h)
        wait_spread(1, h)
        for side in range(2):
            @pl.when(sends[side])
            def _():
                for s in range(UMAX):
                    index = lists[side, s]
                    halo_out[side][h][0, s] = k_all[h][index]
                    halo_out[side][h][1, s] = v_all[h][index]
                halo(side, h).start()

    for side in range(2):
        @pl.when(jnp.logical_not(receives[side]))
        def _():
            for h in range(heads):
                halo_in[side][h][...] = jnp.zeros(halo_in[side][h].shape, halo_in[side][h].dtype)

    scale = math.log2(math.e) / math.sqrt(HEAD_DIM)
    across = (((1,), (1,)), ((), ()))

    def attend(h, r):
        query = q_all[h][r]
        first = jnp.clip(r - REACH, 0, bands - window)
        near = k_all[h][pl.ds(first, window)].reshape(window * tile, HEAD_DIM)
        scores = lax.dot_general(query, near, across, preferred_element_type=jnp.float32)
        parts, value_parts = [], []
        for j in range(window):
            bias = jnp.where(meta[r, first + j] > 0, 0.0, MASKED)
            parts.append(scores[:, j * tile : (j + 1) * tile] + bias)
        for side in range(2):
            for p in range(PICKS):
                at = bands + 2 * PICKS * side + p
                index = meta[r, at]
                bias = jnp.where(meta[r, at + PICKS] > 0, 0.0, MASKED)
                one = lax.dot_general(query, halo_in[side][h][0, index], across, preferred_element_type=jnp.float32)
                parts.append(one + bias)
                value_parts.append((side, index))
        top = functools.reduce(jnp.maximum, parts)
        top = jnp.max(top, axis=1, keepdims=True)
        raised = [jnp.exp2((part - top) * scale) for part in parts]
        total = jnp.sum(functools.reduce(jnp.add, raised), axis=1, keepdims=True)
        raised = [one.astype(jnp.bfloat16) for one in raised]
        near = v_all[h][pl.ds(first, window)].reshape(window * tile, HEAD_DIM)
        result = jnp.dot(jnp.concatenate(raised[:window], axis=1), near, preferred_element_type=jnp.float32)
        for one, (side, index) in zip(raised[window:], value_parts):
            result = result + jnp.dot(one, halo_in[side][h][1, index], preferred_element_type=jnp.float32)
        o_all[h][r] = (result / total).astype(o_all[h].dtype)

    def give_back(h, peer, head_group):
        columns = pl.ds(pl.multiple_of((head_group * heads + h) * HEAD_DIM, HEAD_DIM), HEAD_DIM)
        return pltpu.make_async_remote_copy(
            src_ref=o_all[h].at[peer],
            dst_ref=out.at[:, columns],
            send_sem=o_send.at[h, peer],
            recv_sem=o_recv.at[h, head_group],
            device_id={"space": peer},
            device_id_type=MESH,
        )

    def keep(h):
        columns = pl.ds(pl.multiple_of((me * heads + h) * HEAD_DIM, HEAD_DIM), HEAD_DIM)
        return pltpu.make_async_copy(o_all[h].at[me], out.at[:, columns], o_own.at[h])

    for h in range(heads):
        wait_spread(2, h)
        for side in range(2):
            @pl.when(receives[side])
            def _():
                halo(side, h).wait_recv()

        @pl.loop(0, bands)
        def _(r):
            attend(h, r)

        @pl.loop(1, bands)
        def _(d):
            give_back(h, lax.rem(me + d, bands), me).start()

        keep(h).start()

    for h in range(heads):
        for a in range(3):
            @pl.loop(1, bands)
            def _(d):
                peer = lax.rem(me + d, bands)
                spread(a, h, peer, me).wait_send()

        for side in range(2):
            @pl.when(sends[side])
            def _():
                halo(side, h).wait_send()

        @pl.loop(1, bands)
        def _(d):
            peer = lax.rem(me + d, bands)
            give_back(h, peer, me).wait_send()
            give_back(h, peer, peer).wait_recv()

        keep(h).wait()


def body(queries, keys, values, tile_mask):
    bands = lax.axis_size("space")
    groups = lax.axis_size("tm")
    g = lax.axis_index("tm")
    tile, width = queries.shape
    heads = width // HEAD_DIM // bands
    own = lax.dynamic_slice(tile_mask, (0, g * bands), (bands, bands))
    prior_tiles, prior_picks, prior_live = adjacent(tile_mask, jnp.maximum(g - 1, 0), bands, g > 0)
    next_tiles, next_picks, next_live = adjacent(tile_mask, jnp.minimum(g + 1, groups - 1), bands, g < groups - 1)
    meta = jnp.concatenate([own, prior_picks, prior_live, next_picks, next_live], axis=1)
    for_next = lax.ppermute(prior_tiles, "tm", [(i + 1, i) for i in range(groups - 1)])
    for_prior = lax.ppermute(next_tiles, "tm", [(i, i + 1) for i in range(groups - 1)])
    lists = jnp.stack([for_next, for_prior])
    whole = (bands, tile, HEAD_DIM)
    halo = (2, UMAX, tile, HEAD_DIM)
    dma = pltpu.SemaphoreType.DMA
    return pl.pallas_call(
        functools.partial(kernel, bands, groups, heads),
        out_shape=jax.ShapeDtypeStruct((tile, width), jnp.bfloat16),
        in_specs=[pl.BlockSpec(memory_space=pltpu.SMEM)] * 2 + [pl.BlockSpec(memory_space=pl.ANY)] * 3,
        out_specs=pl.BlockSpec(memory_space=pl.ANY),
        scratch_shapes=[pltpu.VMEM(whole, jnp.bfloat16)] * (4 * heads)
        + [pltpu.VMEM(halo, jnp.bfloat16)] * (4 * heads)
        + [
            dma((3, heads)),
            dma((3, heads, bands)),
            dma((3, heads, bands)),
            dma((2, heads)),
            dma((2, heads)),
            dma((heads,)),
            dma((heads, bands)),
            dma((heads, bands)),
        ],
        compiler_params=pltpu.CompilerParams(
            collective_id=0, has_side_effects=True, vmem_limit_bytes=40 * 1024 * 1024
        ),
    )(meta, lists, queries, keys, values)


def solution(mesh):
    placed = (
        P(("tm", "space"), None),
        P(("tm", "space"), None),
        P(("tm", "space"), None),
        P("tm", None),
    )
    return jax.shard_map(
        body, mesh=mesh, in_specs=placed, out_specs=P(("tm", "space"), None), check_vma=False
    )
```

time: 418 us -> 186 us (0.44)
  the two profiles are of different devices: /device:TPU:25 before, /device:TPU:128 now
where the time goes in v1:
time: 186 us
  Pallas kernels  168 us (90%)
  starting transfers between devices  9.46 us (5%)
  local copies, waits for them, and re-layouts  5.81 us (3%)
    pallas_call x1, Pallas kernels, body(): pl.pallas_call(functools.partial(kernel, bands, groups, heads), out_shape...  168 us
    ppermute x1, starting transfers between devices, body(): lax.ppermute(prior_tiles, 'tm', [(i + 1, i) for i in range(groups - 1)])  7.54 us
    unnamed x9, local copies, waits for them, and re-layouts  5.4 us
  transfers between devices with their start and end apart: 2, of which 1 were waited for; matrix products, arithmetic and copies ran while one was open for 1% of the time, Pallas kernels for 0%

profile of v1, /device:TPU:128, one launch (start us, length us, event | category | flops | bytes accessed | tf_op | source)
XLA Modules:
  0.0 185.5 jit_solution(14015111721443358211)
XLA Ops:
  0.0 0.0 copy-start.3
  0.0 0.8 copy-done.3
  0.8 0.1 fusion.6
  0.9 0.1 select_reduce_fusion.2
  1.0 0.1 select_reduce_fusion.4
  1.1 1.9 %collective-permute-start.1 = (s32[8]{0:T(128)S(1)}, s32[8]{0:T(128)S(1)}, u32[]{:S(2)}, u32[]{:S(2)}) collective-permute-start(s32[8]{0:T(128)S(1)} %select_reduce_fusion.4), channel_id=1, source_target_pairs={{0,16},{16,32},{32,48},{48,64},{64,80},{80,96},{96,112},{112,128},... | collective-permute-start | bytes 104 | tf_op jit(solution)/shard_map/ppermute | solution.py:228
  3.0 0.1 select_reduce_fusion.3
  3.1 0.1 select_reduce_fusion.5
  3.2 7.5 %collective-permute-start = (s32[8]{0:T(128)S(1)}, s32[8]{0:T(128)S(1)}, u32[]{:S(2)}, u32[]{:S(2)}) collective-permute-start(s32[8]{0:T(128)S(1)} %select_reduce_fusion.5), channel_id=1, source_target_pairs={{16,0},{32,16},{48,32},{64,48},{80,64},{96,80},{112,96},{128,112},... | collective-permute-start | bytes 104 | tf_op jit(solution)/shard_map/ppermute | solution.py:227
  10.8 0.1 multiply_reduce_fusion
  11.0 0.2 convert_reduce_fusion.1
  11.2 0.1 copy.6
  11.2 0.2 convert_reduce_fusion
  11.4 0.1 copy.8
  11.5 0.1 copy.5
  11.6 0.1 copy.7
  11.7 0.1 concatenate.3.meta
  11.8 0.0 collective-permute-done.1
  11.8 1.3 collective-permute-done
  13.0 0.0 copy-start
  13.0 1.2 copy-done
  14.3 0.0 copy-start.1
  14.3 1.2 copy-done.1
  15.5 0.0 copy-start.2
  15.5 1.2 copy-done.2
  16.7 167.8 %shard_map.46 = bf16[128,4096]{1,0:T(8,128)(2,1)S(1)} custom-call(s32[16,28]{1,0:T(8,128)S(1)} %concatenate.3.meta, s32[2,8]{1,0:T(2,128)S(1)} %pad_add_fusion.lists, bf16[128,4096]{1,0:T(8,128)(2,1)S(1)} %copy-done, bf16[128,4096]{1,0:T(8,128)(2,1)S(1)} %copy-done.1, bf16[128,4096]{1,0:T(8,128)(2,1)S(1)} %copy-done.2), custom_call_target="tpu_custom_call" | custom-call | tf_op jit(solution)/shard_map/pallas_call | solution.py:233
  184.5 1.0 copy.10
  (8 shorter events, 0.1 us)
Async XLA Ops:
  0.0 0.8 copy-start.3
  1.1 10.7 %collective-permute-start.1 = (s32[8]{0:T(128)S(1)}, s32[8]{0:T(128)S(1)}, u32[]{:S(2)}, u32[]{:S(2)}) collective-permute-start(s32[8]{0:T(128)S(1)} %select_reduce_fusion.4), channel_id=1, source_target_pairs={{0,16},{16,32},{32,48},{48,64},{64,80},{80,96},{96,112},{112,128},... | collective-permute-start | bytes 104 | tf_op jit(solution)/shard_map/ppermute | solution.py:228
  3.2 9.8 %collective-permute-start = (s32[8]{0:T(128)S(1)}, s32[8]{0:T(128)S(1)}, u32[]{:S(2)}, u32[]{:S(2)}) collective-permute-start(s32[8]{0:T(128)S(1)} %select_reduce_fusion.5), channel_id=1, source_target_pairs={{16,0},{32,16},{48,32},{64,48},{80,64},{96,80},{112,96},{128,112},... | collective-permute-start | bytes 104 | tf_op jit(solution)/shard_map/ppermute | solution.py:227
  13.0 1.2 copy-start
  14.3 1.2 copy-start.1
  15.5 1.2 copy-start.2

commit v2 on v1

--- a/solution.py
+++ b/solution.py
@@ -36,13 +36,17 @@
 
 def kernel(
     bands, groups, heads,
-    meta, lists, q_in, k_in, v_in, out,
+    meta, wants, q_in, k_in, v_in, out,
     *scratch,
 ):
     q_all, k_all, v_all, o_all = (scratch[i * heads : (i + 1) * heads] for i in range(4))
     halo_out = [scratch[(4 + i) * heads : (5 + i) * heads] for i in range(2)]
     halo_in = [scratch[(6 + i) * heads : (7 + i) * heads] for i in range(2)]
-    (own_sem, send_sem, recv_sem, halo_send, halo_recv, o_own, o_send, o_recv) = scratch[8 * heads :]
+    near_sum, near_top, near_total = (scratch[(8 + i) * heads : (9 + i) * heads] for i in range(3))
+    (
+        asked, lists, ask_send, ask_recv, ask_own,
+        own_sem, send_sem, recv_sem, halo_send, halo_recv, o_own, o_send, o_recv,
+    ) = scratch[11 * heads :]
     g = lax.axis_index("tm")
     me = lax.axis_index("space")
     tile = q_in.shape[0]
@@ -69,6 +73,23 @@
         copy.start()
 
     pl.semaphore_wait(barrier, bands + 1)
+
+    exists = (g < groups - 1, g > 0)
+
+    def ask(side):
+        return pltpu.make_async_remote_copy(
+            src_ref=wants.at[side],
+            dst_ref=asked[1 - side],
+            send_sem=ask_send.at[side],
+            recv_sem=ask_recv.at[1 - side],
+            device_id={"tm": g + 1 if side == 0 else g - 1},
+            device_id_type=MESH,
+        )
+
+    for side in range(2):
+        @pl.when(exists[side])
+        def _():
+            ask(side).start()
 
     def spread(a, h, peer, source_band):
         source, target = ((k_in, k_all), (v_in, v_all), (q_in, q_all))[a]
@@ -109,23 +130,30 @@
             device_id_type=MESH,
         )
 
-    sends = (g < groups - 1, g > 0)
-    receives = (g > 0, g < groups - 1)
+    def fetch_list(side):
+        return pltpu.make_async_copy(asked[side], lists[side], ask_own.at[side])
+
+    for side in range(2):
+        @pl.when(exists[side])
+        def _():
+            ask(1 - side).wait_recv()
+            fetch_list(side).start()
+            fetch_list(side).wait()
 
     for h in range(heads):
         wait_spread(0, h)
         wait_spread(1, h)
         for side in range(2):
-            @pl.when(sends[side])
+            @pl.when(exists[side])
             def _():
                 for s in range(UMAX):
-                    index = lists[side, s]
+                    index = lists[side][0, s]
                     halo_out[side][h][0, s] = k_all[h][index]
                     halo_out[side][h][1, s] = v_all[h][index]
                 halo(side, h).start()
 
     for side in range(2):
-        @pl.when(jnp.logical_not(receives[side]))
+        @pl.when(jnp.logical_not(exists[1 - side]))
         def _():
             for h in range(heads):
                 halo_in[side][h][...] = jnp.zeros(halo_in[side][h].shape, halo_in[side][h].dtype)
@@ -133,33 +161,47 @@
     scale = math.log2(math.e) / math.sqrt(HEAD_DIM)
     across = (((1,), (1,)), ((), ()))
 
-    def attend(h, r):
-        query = q_all[h][r]
+    def softmax(parts, floor=None):
+        top = jnp.max(functools.reduce(jnp.maximum, parts), axis=1, keepdims=True)
+        if floor is not None:
+            top = jnp.maximum(top, floor)
+        raised = [jnp.exp2((part - top) * scale) for part in parts]
+        total = jnp.sum(functools.reduce(jnp.add, raised), axis=1, keepdims=True)
+        return top, total, [one.astype(jnp.bfloat16) for one in raised]
+
+    def attend_near(h, r):
         first = jnp.clip(r - REACH, 0, bands - window)
         near = k_all[h][pl.ds(first, window)].reshape(window * tile, HEAD_DIM)
-        scores = lax.dot_general(query, near, across, preferred_element_type=jnp.float32)
-        parts, value_parts = [], []
-        for j in range(window):
-            bias = jnp.where(meta[r, first + j] > 0, 0.0, MASKED)
-            parts.append(scores[:, j * tile : (j + 1) * tile] + bias)
+        scores = lax.dot_general(q_all[h][r], near, across, preferred_element_type=jnp.float32)
+        parts = [
+            scores[:, j * tile : (j + 1) * tile] + jnp.where(meta[r, first + j] > 0, 0.0, MASKED)
+            for j in range(window)
+        ]
+        top, total, raised = softmax(parts)
+        near = v_all[h][pl.ds(first, window)].reshape(window * tile, HEAD_DIM)
+        near_sum[h][r] = jnp.dot(jnp.concatenate(raised, axis=1), near, preferred_element_type=jnp.float32)
+        near_top[h][r] = jnp.broadcast_to(top, (tile, HEAD_DIM))
+        near_total[h][r] = jnp.broadcast_to(total, (tile, HEAD_DIM))
+
+    def attend_far(h, r):
+        key_parts, value_parts, biases = [], [], []
         for side in range(2):
             for p in range(PICKS):
                 at = bands + 2 * PICKS * side + p
                 index = meta[r, at]
-                bias = jnp.where(meta[r, at + PICKS] > 0, 0.0, MASKED)
-                one = lax.dot_general(query, halo_in[side][h][0, index], across, preferred_element_type=jnp.float32)
-                parts.append(one + bias)
-                value_parts.append((side, index))
-        top = functools.reduce(jnp.maximum, parts)
-        top = jnp.max(top, axis=1, keepdims=True)
-        raised = [jnp.exp2((part - top) * scale) for part in parts]
-        total = jnp.sum(functools.reduce(jnp.add, raised), axis=1, keepdims=True)
-        raised = [one.astype(jnp.bfloat16) for one in raised]
-        near = v_all[h][pl.ds(first, window)].reshape(window * tile, HEAD_DIM)
-        result = jnp.dot(jnp.concatenate(raised[:window], axis=1), near, preferred_element_type=jnp.float32)
-        for one, (side, index) in zip(raised[window:], value_parts):
-            result = result + jnp.dot(one, halo_in[side][h][1, index], preferred_element_type=jnp.float32)
-        o_all[h][r] = (result / total).astype(o_all[h].dtype)
+                biases.append(jnp.where(meta[r, at + PICKS] > 0, 0.0, MASKED))
+                key_parts.append(halo_in[side][h][0, index])
+                value_parts.append(halo_in[side][h][1, index])
+        far = jnp.concatenate(key_parts, axis=0)
+        scores = lax.dot_general(q_all[h][r], far, across, preferred_element_type=jnp.float32)
+        parts = [scores[:, j * tile : (j + 1) * tile] + bias for j, bias in enumerate(biases)]
+        before = near_top[h][r][:, :1]
+        top, total, raised = softmax(parts, before)
+        kept = jnp.exp2((before - top) * scale)
+        total = near_total[h][r][:, :1] * kept + total
+        far = jnp.concatenate(value_parts, axis=0)
+        result = jnp.dot(jnp.concatenate(raised, axis=1), far, preferred_element_type=jnp.float32)
+        o_all[h][r] = ((near_sum[h][r] * kept + result) / total).astype(o_all[h].dtype)
 
     def give_back(h, peer, head_group):
         columns = pl.ds(pl.multiple_of((head_group * heads + h) * HEAD_DIM, HEAD_DIM), HEAD_DIM)
@@ -178,18 +220,27 @@
 
     for h in range(heads):
         wait_spread(2, h)
+
+        @pl.loop(0, bands, unroll=2)
+        def _(r):
+            attend_near(h, r)
+
+    for h in range(heads):
         for side in range(2):
-            @pl.when(receives[side])
+            @pl.when(exists[1 - side])
             def _():
                 halo(side, h).wait_recv()
 
-        @pl.loop(0, bands)
-        def _(r):
-            attend(h, r)
-
-        @pl.loop(1, bands)
-        def _(d):
-            give_back(h, lax.rem(me + d, bands), me).start()
+        @pl.loop(0, bands // 2)
+        def _(i):
+            places = [lax.rem(me + 2 * i + j + 1, bands) for j in range(2)]
+            for r in places:
+                attend_far(h, r)
+            give_back(h, places[0], me).start()
+
+            @pl.when(i < bands // 2 - 1)
+            def _():
+                give_back(h, places[1], me).start()
 
         keep(h).start()
 
@@ -201,9 +252,11 @@
                 spread(a, h, peer, me).wait_send()
 
         for side in range(2):
-            @pl.when(sends[side])
+            @pl.when(exists[side])
             def _():
                 halo(side, h).wait_send()
+                if h == 0:
+                    ask(side).wait_send()
 
         @pl.loop(1, bands)
         def _(d):
@@ -224,20 +277,24 @@
     prior_tiles, prior_picks, prior_live = adjacent(tile_mask, jnp.maximum(g - 1, 0), bands, g > 0)
     next_tiles, next_picks, next_live = adjacent(tile_mask, jnp.minimum(g + 1, groups - 1), bands, g < groups - 1)
     meta = jnp.concatenate([own, prior_picks, prior_live, next_picks, next_live], axis=1)
-    for_next = lax.ppermute(prior_tiles, "tm", [(i + 1, i) for i in range(groups - 1)])
-    for_prior = lax.ppermute(next_tiles, "tm", [(i, i + 1) for i in range(groups - 1)])
-    lists = jnp.stack([for_next, for_prior])
+    wants = jnp.zeros((2, 8, 128), jnp.int32).at[:, 0, :UMAX].set(jnp.stack([next_tiles, prior_tiles]))
     whole = (bands, tile, HEAD_DIM)
     halo = (2, UMAX, tile, HEAD_DIM)
     dma = pltpu.SemaphoreType.DMA
     return pl.pallas_call(
         functools.partial(kernel, bands, groups, heads),
         out_shape=jax.ShapeDtypeStruct((tile, width), jnp.bfloat16),
-        in_specs=[pl.BlockSpec(memory_space=pltpu.SMEM)] * 2 + [pl.BlockSpec(memory_space=pl.ANY)] * 3,
+        in_specs=[pl.BlockSpec(memory_space=pltpu.SMEM), pl.BlockSpec(memory_space=pltpu.VMEM)]
+        + [pl.BlockSpec(memory_space=pl.ANY)] * 3,
         out_specs=pl.BlockSpec(memory_space=pl.ANY),
         scratch_shapes=[pltpu.VMEM(whole, jnp.bfloat16)] * (4 * heads)
         + [pltpu.VMEM(halo, jnp.bfloat16)] * (4 * heads)
+        + [pltpu.VMEM(whole, jnp.float32)] * (3 * heads)
+        + [[pltpu.VMEM((8, 128), jnp.int32)] * 2, [pltpu.SMEM((8, 128), jnp.int32)] * 2]
         + [
+            dma((2,)),
+            dma((2,)),
+            dma((2,)),
             dma((3, heads)),
             dma((3, heads, bands)),
             dma((3, heads, bands)),
@@ -248,9 +305,9 @@
             dma((heads, bands)),
         ],
         compiler_params=pltpu.CompilerParams(
-            collective_id=0, has_side_effects=True, vmem_limit_bytes=40 * 1024 * 1024
+            collective_id=0, has_side_effects=True, vmem_limit_bytes=56 * 1024 * 1024
         ),
-    )(meta, lists, queries, keys, values)
+    )(meta, wants, queries, keys, values)
 
 
 def solution(mesh):

time: 186 us -> 166 us (0.89)
  the two profiles are of different devices: /device:TPU:128 before, /device:TPU:8 now
where the time goes in v2:
time: 166 us
  Pallas kernels  160 us (96%)
  local copies, waits for them, and re-layouts  4.65 us (3%)
    pallas_call x1, Pallas kernels, body(): pl.pallas_call(functools.partial(kernel, bands, groups, heads), out_shape...  160 us

profile of v2, /device:TPU:8, one launch (start us, length us, event | category | flops | bytes accessed | tf_op | source)
XLA Modules:
  0.0 165.5 jit_solution(12313546934689418655)
XLA Ops:
  0.0 0.0 copy-start
  0.0 0.7 copy-done
  0.8 0.1 fusion.6
  0.9 0.1 select_reduce_fusion.2
  1.0 0.1 select_reduce_fusion.5
  1.1 0.1 select_reduce_fusion.4
  1.2 0.1 multiply_reduce_fusion
  1.4 0.2 convert_reduce_fusion
  1.6 0.2 convert_reduce_fusion.1
  1.8 0.1 copy.7
  1.9 0.1 copy.9
  1.9 0.6 scatter.4.wants
  2.5 0.1 copy.6
  2.6 0.1 copy.8
  2.7 0.7 concatenate.5.meta
  3.4 159.9 %shard_map.46 = bf16[128,4096]{1,0:T(8,128)(2,1)} custom-call(s32[16,28]{1,0:T(8,128)} %concatenate.5.meta, s32[2,8,128]{2,1,0:T(8,128)} %scatter.4.wants, bf16[128,4096]{1,0:T(8,128)(2,1)} %q_in.1, bf16[128,4096]{1,0:T(8,128)(2,1)} %k_in.1, bf16[128,4096]{1,0:T(8,128)(2,1)} %v_in.1), custom_call_target="tpu_custom_call" | custom-call | tf_op jit(solution)/shard_map/pallas_call | solution.py:284
  163.2 2.3 %copy.12 = bf16[128,4096]{1,0:T(8,128)(2,1)} copy(bf16[128,4096]{1,0:T(8,128)(2,1)} %shard_map.46) | data formatting | bytes 2097152
  (7 shorter events, 0.0 us)
Async XLA Ops:
  0.0 0.8 copy-start

commit v3 on v2

v3 whole, which is shorter than its diff:
```python
import functools
import math

import jax
import jax.numpy as jnp
from jax import lax
from jax.experimental import pallas as pl
from jax.experimental.pallas import tpu as pltpu
from jax.sharding import PartitionSpec as P

HEAD_DIM = 128
REACH = 4
UMAX = 8
PICKS = 3
LANES = 128
MASKED = -1e30
MESH = pl.DeviceIdType.MESH


def plan(mask, g, bands):
    total = mask.shape[1]
    near = pltpu.roll(mask, lax.rem(2 * total - (g - 1) * bands, total), 1)[:, :LANES]
    lane = lax.broadcasted_iota(jnp.int32, near.shape, 1)
    list_lane = lax.broadcasted_iota(jnp.int32, (8, LANES), 1)
    used = jnp.max(near, axis=0, keepdims=True)
    packed = jnp.where(lane < 3 * bands, near, 0)
    lists = []
    for side, base in enumerate((2 * bands, 0)):
        place = jnp.zeros((1, LANES), jnp.int32)
        order = jnp.zeros_like(near)
        picks = [jnp.zeros_like(near) for _ in range(PICKS)]
        tiles = jnp.zeros((8, LANES), jnp.int32)
        for c in range(bands):
            taken = jnp.broadcast_to(near[:, base + c : base + c + 1], near.shape)
            wanted = jnp.broadcast_to(used[:, base + c : base + c + 1], (1, LANES))
            tiles = tiles + jnp.where((wanted > 0) & (list_lane == place), c, 0)
            for p in range(PICKS):
                picks[p] = picks[p] + jnp.where((taken > 0) & (order == p), place, 0)
            place = place + wanted
            order = order + taken
        at = 3 * bands + 2 * PICKS * side
        for p in range(PICKS):
            packed = jnp.where(lane == at + p, picks[p], packed)
            packed = jnp.where(lane == at + PICKS + p, jnp.where(order > p, 1, 0), packed)
        lists.append(tiles)
    return packed, lists


def kernel(bands, groups, heads, mask_in, q_in, k_in, v_in, out, *scratch):
    q_all, k_all, v_all, o_all = (scratch[i * heads : (i + 1) * heads] for i in range(4))
    halo_out = [scratch[(4 + i) * heads : (5 + i) * heads] for i in range(2)]
    halo_in = [scratch[(6 + i) * heads : (7 + i) * heads] for i in range(2)]
    near_sum, near_top, near_total = (scratch[(8 + i) * heads : (9 + i) * heads] for i in range(3))
    (
        mask, packed, meta, wants, asked, lists,
        mask_sem, meta_sem, ask_send, ask_recv, ask_own,
        own_sem, send_sem, recv_sem, halo_send, halo_recv, o_own, o_send, o_recv,
    ) = scratch[11 * heads :]
    g = lax.axis_index("tm")
    me = lax.axis_index("space")
    tile = q_in.shape[0]
    window = min(2 * REACH + 1, bands)
    exists = (g < groups - 1, g > 0)
    moved = ((k_in, k_all), (v_in, v_all), (q_in, q_all))

    barrier = pltpu.get_barrier_semaphore()

    @pl.loop(1, bands)
    def _(d):
        pl.semaphore_signal(barrier, inc=1, device_id={"space": lax.rem(me + d, bands)}, device_id_type=MESH)

    for step in (1, groups - 1):
        pl.semaphore_signal(barrier, inc=1, device_id={"tm": lax.rem(g + step, groups)}, device_id_type=MESH)

    def head_columns(owner, h):
        return pl.ds(pl.multiple_of((owner * heads + h) * HEAD_DIM, HEAD_DIM), HEAD_DIM)

    fetch_mask = pltpu.make_async_copy(mask_in, mask, mask_sem)
    fetch_mask.start()

    def own_copy(a, h):
        source, target = moved[a]
        return pltpu.make_async_copy(source.at[:, head_columns(me, h)], target[h].at[me], own_sem.at[a, h])

    for h in range(heads):
        for a in range(3):
            own_copy(a, h).start()

    fetch_mask.wait()
    packed[...], found = plan(mask[...], g, bands)
    for side in range(2):
        wants[side][...] = found[side]
    fetch_meta = pltpu.make_async_copy(packed, meta, meta_sem)
    fetch_meta.start()

    pl.semaphore_wait(barrier, bands + 1)

    def ask(side):
        return pltpu.make_async_remote_copy(
            src_ref=wants[side],
            dst_ref=asked[1 - side],
            send_sem=ask_send.at[side],
            recv_sem=ask_recv.at[1 - side],
            device_id={"tm": g + 1 if side == 0 else g - 1},
            device_id_type=MESH,
        )

    for side in range(2):
        @pl.when(exists[side])
        def _():
            ask(side).start()

    def spread(a, h, peer):
        source, target = moved[a]
        return pltpu.make_async_remote_copy(
            src_ref=source.at[:, head_columns(peer, h)],
            dst_ref=target[h].at[me],
            send_sem=send_sem.at[a, h],
            recv_sem=recv_sem.at[a, h],
            device_id={"space": peer},
            device_id_type=MESH,
        )

    def start_spread(a, h):
        @pl.loop(1, bands)
        def _(d):
            spread(a, h, lax.rem(me + d, bands)).start()

    def wait_bytes(buffer, sem):
        part = buffer.at[pl.ds(0, bands - 1)]
        pltpu.make_async_copy(part, part, sem).wait()

    def wait_spread(a, h):
        wait_bytes(moved[a][1][h], recv_sem.at[a, h])
        own_copy(a, h).wait()

    for a, h in [(a, h) for h in range(heads) for a in (0, 1)] + [(2, h) for h in range(heads)]:
        start_spread(a, h)

    def halo(side, h):
        return pltpu.make_async_remote_copy(
            src_ref=halo_out[side][h],
            dst_ref=halo_in[side][h],
            send_sem=halo_send.at[side, h],
            recv_sem=halo_recv.at[side, h],
            device_id={"tm": g + 1 if side == 0 else g - 1},
            device_id_type=MESH,
        )

    def fetch_list(side):
        return pltpu.make_async_copy(asked[side], lists[side], ask_own.at[side])

    for side in range(2):
        @pl.when(jnp.logical_not(exists[1 - side]))
        def _():
            for h in range(heads):
                halo_in[side][h][...] = jnp.zeros(halo_in[side][h].shape, halo_in[side][h].dtype)

    fetch_meta.wait()
    for side in range(2):
        @pl.when(exists[side])
        def _():
            ask(1 - side).wait_recv()
            fetch_list(side).start()

    for side in range(2):
        @pl.when(exists[side])
        def _():
            fetch_list(side).wait()

    def fill_halo(h):
        wait_spread(0, h)
        wait_spread(1, h)
        for side in range(2):
            @pl.when(exists[side])
            def _():
                for s in range(UMAX):
                    index = lists[side][0, s]
                    halo_out[side][h][0, s] = k_all[h][index]
                    halo_out[side][h][1, s] = v_all[h][index]

    def each_side(action, h, receive=False):
        for side in range(2):
            @pl.when(exists[1 - side if receive else side])
            def _():
                action(halo(side, h))

    scale = math.log2(math.e) / math.sqrt(HEAD_DIM)
    across = (((1,), (1,)), ((), ()))

    def softmax(parts, floor=None):
        top = jnp.max(functools.reduce(jnp.maximum, parts), axis=1, keepdims=True)
        if floor is not None:
            top = jnp.maximum(top, floor)
        raised = [jnp.exp2((part - top) * scale) for part in parts]
        total = jnp.sum(functools.reduce(jnp.add, raised), axis=1, keepdims=True)
        return top, total, [one.astype(jnp.bfloat16) for one in raised]

    def attend_near(h, r):
        first = jnp.clip(r - REACH, 0, bands - window)
        near = k_all[h][pl.ds(first, window)].reshape(window * tile, HEAD_DIM)
        scores = lax.dot_general(q_all[h][r], near, across, preferred_element_type=jnp.float32)
        parts = [
            scores[:, j * tile : (j + 1) * tile] + jnp.where(meta[r, bands + first + j] > 0, 0.0, MASKED)
            for j in range(window)
        ]
        top, total, raised = softmax(parts)
        near = v_all[h][pl.ds(first, window)].reshape(window * tile, HEAD_DIM)
        near_sum[h][r] = jnp.dot(jnp.concatenate(raised, axis=1), near, preferred_element_type=jnp.float32)
        near_top[h][r] = jnp.broadcast_to(top, (tile, HEAD_DIM))
        near_total[h][r] = jnp.broadcast_to(total, (tile, HEAD_DIM))

    def attend_far(h, r):
        key_parts, value_parts, biases = [], [], []
        for side in range(2):
            for p in range(PICKS):
                at = 3 * bands + 2 * PICKS * (1 - side) + p
                index = meta[r, at]
                biases.append(jnp.where(meta[r, at + PICKS] > 0, 0.0, MASKED))
                key_parts.append(halo_in[side][h][0, index])
                value_parts.append(halo_in[side][h][1, index])
        far = jnp.concatenate(key_parts, axis=0)
        scores = lax.dot_general(q_all[h][r], far, across, preferred_element_type=jnp.float32)
        parts = [scores[:, j * tile : (j + 1) * tile] + bias for j, bias in enumerate(biases)]
        before = near_top[h][r][:, :1]
        top, total, raised = softmax(parts, before)
        kept = jnp.exp2((before - top) * scale)
        total = near_total[h][r][:, :1] * kept + total
        far = jnp.concatenate(value_parts, axis=0)
        result = jnp.dot(jnp.concatenate(raised, axis=1), far, preferred_element_type=jnp.float32)
        o_all[h][r] = ((near_sum[h][r] * kept + result) / total).astype(o_all[h].dtype)

    def give_back(h, peer):
        return pltpu.make_async_remote_copy(
            src_ref=o_all[h].at[peer],
            dst_ref=out.at[:, head_columns(me, h)],
            send_sem=o_send.at[h],
            recv_sem=o_recv.at[h],
            device_id={"space": peer},
            device_id_type=MESH,
        )

    def keep(h):
        return pltpu.make_async_copy(o_all[h].at[me], out.at[:, head_columns(me, h)], o_own.at[h])

    def near_loop(h):
        wait_spread(2, h)

        @pl.loop(0, bands, unroll=2)
        def _(r):
            attend_near(h, r)

    def far_loop(h):
        each_side(lambda copy: copy.wait_recv(), h, receive=True)

        @pl.loop(0, bands // 2)
        def _(i):
            places = [lax.rem(me + 2 * i + j + 1, bands) for j in range(2)]
            for r in places:
                attend_far(h, r)
            give_back(h, places[0]).start()

            @pl.when(i < bands // 2 - 1)
            def _():
                give_back(h, places[1]).start()

        keep(h).start()

    for h in range(heads):
        fill_halo(h)
        each_side(lambda copy: copy.start(), h)
    for h in range(heads):
        near_loop(h)
    for h in range(heads):
        far_loop(h)
    for h in range(heads):
        each_side(lambda copy: copy.wait_send(), h)

    for h in range(heads):
        for a in range(3):
            wait_bytes(moved[a][1][h], send_sem.at[a, h])
        for side in range(2):
            @pl.when(exists[side])
            def _():
                if h == 0:
                    ask(side).wait_send()
        wait_bytes(o_all[h], o_send.at[h])
        wait_bytes(o_all[h], o_recv.at[h])
        keep(h).wait()


def body(queries, keys, values, tile_mask):
    bands = lax.axis_size("space")
    groups = lax.axis_size("tm")
    tile, width = queries.shape
    heads = width // HEAD_DIM // bands
    whole = (bands, tile, HEAD_DIM)
    halo = (2, UMAX, tile, HEAD_DIM)
    dma = pltpu.SemaphoreType.DMA
    return pl.pallas_call(
        functools.partial(kernel, bands, groups, heads),
        out_shape=jax.ShapeDtypeStruct((tile, width), jnp.bfloat16),
        in_specs=[pl.BlockSpec(memory_space=pl.ANY)] * 4,
        out_specs=pl.BlockSpec(memory_space=pl.ANY),
        scratch_shapes=[pltpu.VMEM(whole, jnp.bfloat16)] * (4 * heads)
        + [pltpu.VMEM(halo, jnp.bfloat16)] * (4 * heads)
        + [pltpu.VMEM(whole, jnp.float32)] * (3 * heads)
        + [
            pltpu.VMEM(tile_mask.shape, jnp.int32),
            pltpu.VMEM((bands, LANES), jnp.int32),
            pltpu.SMEM((bands, LANES), jnp.int32),
            [pltpu.VMEM((8, LANES), jnp.int32)] * 2,
            [pltpu.VMEM((8, LANES), jnp.int32)] * 2,
            [pltpu.SMEM((8, LANES), jnp.int32)] * 2,
            dma,
            dma,
            dma((2,)),
            dma((2,)),
            dma((2,)),
            dma((3, heads)),
            dma((3, heads)),
            dma((3, heads)),
            dma((2, heads)),
            dma((2, heads)),
            dma((heads,)),
            dma((heads,)),
            dma((heads,)),
        ],
        compiler_params=pltpu.CompilerParams(
            collective_id=0, has_side_effects=True, vmem_limit_bytes=56 * 1024 * 1024
        ),
    )(tile_mask, queries, keys, values)


def solution(mesh):
    placed = (
        P(("tm", "space"), None),
        P(("tm", "space"), None),
        P(("tm", "space"), None),
        P("tm", None),
    )
    return jax.shard_map(
        body, mesh=mesh, in_specs=placed, out_specs=P(("tm", "space"), None), check_vma=False
    )
```

time: 166 us -> 159 us (0.958)
  Pallas kernels: 160 us -> 157 us
  local copies, waits for them, and re-layouts: 4.65 us -> 2.29 us
    pallas_call x1, Pallas kernels: 160 us -> 157 us  [body(): pl.pallas_call(functools.partial(kernel, bands, groups, heads), out_shape...]
where the time goes in v3:
time: 159 us
  Pallas kernels  157 us (99%)
  local copies, waits for them, and re-layouts  2.29 us (1%)
    pallas_call x1, Pallas kernels, body(): pl.pallas_call(functools.partial(kernel, bands, groups, heads), out_shape...  157 us

profile of v3, /device:TPU:8, one launch (start us, length us, event | category | flops | bytes accessed | tf_op | source)
XLA Modules:
  0.0 159.1 jit_solution(4753567853491664961)
XLA Ops:
  0.0 156.8 %shard_map.46 = bf16[128,4096]{1,0:T(8,128)(2,1)} custom-call(s32[16,512]{1,0:T(8,128)} %mask_in.1, bf16[128,4096]{1,0:T(8,128)(2,1)} %q_in.1, bf16[128,4096]{1,0:T(8,128)(2,1)} %k_in.1, bf16[128,4096]{1,0:T(8,128)(2,1)} %v_in.1), custom_call_target="tpu_custom_call" | custom-call | tf_op jit(solution)/shard_map/pallas_call | solution.py:300
  156.8 2.3 %copy.6 = bf16[128,4096]{1,0:T(8,128)(2,1)} copy(bf16[128,4096]{1,0:T(8,128)(2,1)} %shard_map.46) | data formatting | bytes 2097152

commit v4 on v3

--- a/solution.py
+++ b/solution.py
@@ -64,6 +64,8 @@
     moved = ((k_in, k_all), (v_in, v_all), (q_in, q_all))
 
     barrier = pltpu.get_barrier_semaphore()
+    fetch_mask = pltpu.make_async_copy(mask_in, mask, mask_sem)
+    fetch_mask.start()
 
     @pl.loop(1, bands)
     def _(d):
@@ -72,26 +74,18 @@
     for step in (1, groups - 1):
         pl.semaphore_signal(barrier, inc=1, device_id={"tm": lax.rem(g + step, groups)}, device_id_type=MESH)
 
+    def place(i):
+        half, low = lax.rem(me // 2, 2), lax.rem(me, 2)
+        other = jnp.where(i < bands // 2, 1 - half, half)
+        x = lax.rem(me // 4 + lax.rem(i, bands // 2) // 2, bands // 4)
+        return x * 4 + other * 2 + lax.rem(low + i, 2)
+
     def head_columns(owner, h):
         return pl.ds(pl.multiple_of((owner * heads + h) * HEAD_DIM, HEAD_DIM), HEAD_DIM)
-
-    fetch_mask = pltpu.make_async_copy(mask_in, mask, mask_sem)
-    fetch_mask.start()
 
     def own_copy(a, h):
         source, target = moved[a]
         return pltpu.make_async_copy(source.at[:, head_columns(me, h)], target[h].at[me], own_sem.at[a, h])
-
-    for h in range(heads):
-        for a in range(3):
-            own_copy(a, h).start()
-
-    fetch_mask.wait()
-    packed[...], found = plan(mask[...], g, bands)
-    for side in range(2):
-        wants[side][...] = found[side]
-    fetch_meta = pltpu.make_async_copy(packed, meta, meta_sem)
-    fetch_meta.start()
 
     pl.semaphore_wait(barrier, bands + 1)
 
@@ -104,11 +98,6 @@
             device_id={"tm": g + 1 if side == 0 else g - 1},
             device_id_type=MESH,
         )
-
-    for side in range(2):
-        @pl.when(exists[side])
-        def _():
-            ask(side).start()
 
     def spread(a, h, peer):
         source, target = moved[a]
@@ -122,9 +111,13 @@
         )
 
     def start_spread(a, h):
-        @pl.loop(1, bands)
-        def _(d):
-            spread(a, h, lax.rem(me + d, bands)).start()
+        @pl.loop(0, bands // 2)
+        def _(i):
+            spread(a, h, place(i)).start()
+
+        @pl.loop(bands // 2 + 1, bands)
+        def _(i):
+            spread(a, h, place(i)).start()
 
     def wait_bytes(buffer, sem):
         part = buffer.at[pl.ds(0, bands - 1)]
@@ -134,13 +127,33 @@
         wait_bytes(moved[a][1][h], recv_sem.at[a, h])
         own_copy(a, h).wait()
 
-    for a, h in [(a, h) for h in range(heads) for a in (0, 1)] + [(2, h) for h in range(heads)]:
-        start_spread(a, h)
-
-    def halo(side, h):
+    def sent(a, h):
+        wait_bytes(moved[a][1][h], send_sem.at[a, h])
+
+    start_spread(0, 0)
+    start_spread(1, 0)
+    start_spread(0, 1)
+    start_spread(1, 1)
+    for h in range(heads):
+        for a in range(3):
+            own_copy(a, h).start()
+
+    fetch_mask.wait()
+    packed[...], found = plan(mask[...], g, bands)
+    for side in range(2):
+        wants[side][...] = found[side]
+    fetch_meta = pltpu.make_async_copy(packed, meta, meta_sem)
+    fetch_meta.start()
+
+    for side in range(2):
+        @pl.when(exists[side])
+        def _():
+            ask(side).start()
+
+    def halo(side, h, s=None):
         return pltpu.make_async_remote_copy(
-            src_ref=halo_out[side][h],
-            dst_ref=halo_in[side][h],
+            src_ref=halo_out[side][h] if s is None else halo_out[side][h].at[:, s],
+            dst_ref=halo_in[side][h] if s is None else halo_in[side][h].at[:, s],
             send_sem=halo_send.at[side, h],
             recv_sem=halo_recv.at[side, h],
             device_id={"tm": g + 1 if side == 0 else g - 1},
@@ -168,7 +181,7 @@
         def _():
             fetch_list(side).wait()
 
-    def fill_halo(h):
+    def fill_halo(h, at_once=True):
         wait_spread(0, h)
         wait_spread(1, h)
         for side in range(2):
@@ -178,6 +191,15 @@
                     index = lists[side][0, s]
                     halo_out[side][h][0, s] = k_all[h][index]
                     halo_out[side][h][1, s] = v_all[h][index]
+                    if at_once:
+                        halo(side, h, s).start()
+
+    def start_halo(h):
+        for side in range(2):
+            @pl.when(exists[side])
+            def _():
+                for s in range(UMAX):
+                    halo(side, h, s).start()
 
     def each_side(action, h, receive=False):
         for side in range(2):
@@ -255,30 +277,36 @@
 
         @pl.loop(0, bands // 2)
         def _(i):
-            places = [lax.rem(me + 2 * i + j + 1, bands) for j in range(2)]
+            places = [place(2 * i + j) for j in range(2)]
             for r in places:
                 attend_far(h, r)
-            give_back(h, places[0]).start()
-
-            @pl.when(i < bands // 2 - 1)
-            def _():
-                give_back(h, places[1]).start()
+
+            @pl.when(i != bands // 4)
+            def _():
+                give_back(h, places[0]).start()
+
+            give_back(h, places[1]).start()
 
         keep(h).start()
 
+    sent(0, 0)
+    sent(1, 0)
+    sent(0, 1)
+    sent(1, 1)
+    start_spread(2, 0)
+    start_spread(2, 1)
+    fill_halo(0)
+    fill_halo(1)
+    near_loop(0)
+    near_loop(1)
+    far_loop(0)
+    far_loop(1)
+    each_side(lambda copy: copy.wait_send(), 0)
+    each_side(lambda copy: copy.wait_send(), 1)
+    sent(2, 0)
+    sent(2, 1)
+
     for h in range(heads):
-        fill_halo(h)
-        each_side(lambda copy: copy.start(), h)
-    for h in range(heads):
-        near_loop(h)
-    for h in range(heads):
-        far_loop(h)
-    for h in range(heads):
-        each_side(lambda copy: copy.wait_send(), h)
-
-    for h in range(heads):
-        for a in range(3):
-            wait_bytes(moved[a][1][h], send_sem.at[a, h])
         for side in range(2):
             @pl.when(exists[side])
             def _():
@@ -299,8 +327,8 @@
     dma = pltpu.SemaphoreType.DMA
     return pl.pallas_call(
         functools.partial(kernel, bands, groups, heads),
-        out_shape=jax.ShapeDtypeStruct((tile, width), jnp.bfloat16),
-        in_specs=[pl.BlockSpec(memory_space=pl.ANY)] * 4,
+        out_shape=pltpu.VMEM((tile, width), jnp.bfloat16),
+        in_specs=[pl.BlockSpec(memory_space=pltpu.HBM)] * 4,
         out_specs=pl.BlockSpec(memory_space=pl.ANY),
         scratch_shapes=[pltpu.VMEM(whole, jnp.bfloat16)] * (4 * heads)
         + [pltpu.VMEM(halo, jnp.bfloat16)] * (4 * heads)

time: 159 us -> 153 us (0.962)
  the two profiles are of different devices: /device:TPU:8 before, /device:TPU:65 now
where the time goes in v4:
time: 153 us
  Pallas kernels  152 us (99%)
    pallas_call x1, Pallas kernels, body(): pl.pallas_call(functools.partial(kernel, bands, groups, heads), out_shape...  152 us

profile of v4, /device:TPU:65, one launch (start us, length us, event | category | flops | bytes accessed | tf_op | source)
XLA Modules:
  0.0 153.1 jit_solution(3790859937963494959)
XLA Ops:
  0.0 152.1 %shard_map.46 = bf16[128,4096]{1,0:T(8,128)(2,1)S(1)} custom-call(s32[16,512]{1,0:T(8,128)} %mask_in.1, bf16[128,4096]{1,0:T(8,128)(2,1)} %q_in.1, bf16[128,4096]{1,0:T(8,128)(2,1)} %k_in.1, bf16[128,4096]{1,0:T(8,128)(2,1)} %v_in.1), custom_call_target="tpu_custom_call" | custom-call | tf_op jit(solution)/shard_map/pallas_call | solution.py:328
  152.1 1.0 copy.6

commit v5 on v4

--- a/solution.py
+++ b/solution.py
@@ -14,6 +14,7 @@
 PICKS = 3
 LANES = 128
 MASKED = -1e30
+RUN = 8
 MESH = pl.DeviceIdType.MESH
 
 
@@ -60,7 +61,9 @@
     me = lax.axis_index("space")
     tile = q_in.shape[0]
     window = min(2 * REACH + 1, bands)
-    exists = (g < groups - 1, g > 0)
+    even = lax.rem(g, 2) == 0
+    beside = (jnp.where(even, g + 1, g - 1), jnp.where(even, g - 1, g + 1))
+    exists = (g >= 0, (beside[1] >= 0) & (beside[1] < groups))
     moved = ((k_in, k_all), (v_in, v_all), (q_in, q_all))
 
     barrier = pltpu.get_barrier_semaphore()
@@ -70,9 +73,6 @@
     @pl.loop(1, bands)
     def _(d):
         pl.semaphore_signal(barrier, inc=1, device_id={"space": lax.rem(me + d, bands)}, device_id_type=MESH)
-
-    for step in (1, groups - 1):
-        pl.semaphore_signal(barrier, inc=1, device_id={"tm": lax.rem(g + step, groups)}, device_id_type=MESH)
 
     def place(i):
         half, low = lax.rem(me // 2, 2), lax.rem(me, 2)
@@ -87,15 +87,23 @@
         source, target = moved[a]
         return pltpu.make_async_copy(source.at[:, head_columns(me, h)], target[h].at[me], own_sem.at[a, h])
 
-    pl.semaphore_wait(barrier, bands + 1)
+    late_left = (g > 0) & even & (lax.rem(g, RUN) != 0)
+    late_right = (g < groups - 1) & (even | (lax.rem(g, RUN) == RUN - 1))
+    at_entry = late_left.astype(jnp.int32) + late_right.astype(jnp.int32)
+    pl.semaphore_wait(barrier, bands - 1 + at_entry)
+
+    for side in range(2):
+        @pl.when(exists[side])
+        def _():
+            pl.semaphore_signal(barrier, inc=1, device_id={"tm": beside[side]}, device_id_type=MESH)
 
     def ask(side):
         return pltpu.make_async_remote_copy(
             src_ref=wants[side],
-            dst_ref=asked[1 - side],
+            dst_ref=asked[side],
             send_sem=ask_send.at[side],
-            recv_sem=ask_recv.at[1 - side],
-            device_id={"tm": g + 1 if side == 0 else g - 1},
+            recv_sem=ask_recv.at[side],
+            device_id={"tm": beside[side]},
             device_id_type=MESH,
         )
 
@@ -141,9 +149,15 @@
     fetch_mask.wait()
     packed[...], found = plan(mask[...], g, bands)
     for side in range(2):
-        wants[side][...] = found[side]
+        wants[side][...] = jnp.where(even, found[side], found[1 - side])
     fetch_meta = pltpu.make_async_copy(packed, meta, meta_sem)
     fetch_meta.start()
+
+    to_come = 1 + exists[1].astype(jnp.int32) - at_entry
+
+    @pl.when(to_come > 0)
+    def _():
+        pl.semaphore_wait(barrier, to_come)
 
     for side in range(2):
         @pl.when(exists[side])
@@ -156,24 +170,23 @@
             dst_ref=halo_in[side][h] if s is None else halo_in[side][h].at[:, s],
             send_sem=halo_send.at[side, h],
             recv_sem=halo_recv.at[side, h],
-            device_id={"tm": g + 1 if side == 0 else g - 1},
+            device_id={"tm": beside[side]},
             device_id_type=MESH,
         )
 
     def fetch_list(side):
         return pltpu.make_async_copy(asked[side], lists[side], ask_own.at[side])
 
-    for side in range(2):
-        @pl.when(jnp.logical_not(exists[1 - side]))
-        def _():
-            for h in range(heads):
-                halo_in[side][h][...] = jnp.zeros(halo_in[side][h].shape, halo_in[side][h].dtype)
+    @pl.when(jnp.logical_not(exists[1]))
+    def _():
+        for h in range(heads):
+            halo_in[1][h][...] = jnp.zeros(halo_in[1][h].shape, halo_in[1][h].dtype)
 
     fetch_meta.wait()
     for side in range(2):
         @pl.when(exists[side])
         def _():
-            ask(1 - side).wait_recv()
+            ask(side).wait_recv()
             fetch_list(side).start()
 
     for side in range(2):
@@ -181,31 +194,17 @@
         def _():
             fetch_list(side).wait()
 
-    def fill_halo(h, at_once=True):
+    def fill_halo(h):
         wait_spread(0, h)
         wait_spread(1, h)
-        for side in range(2):
+        for side in (1, 0):
             @pl.when(exists[side])
             def _():
                 for s in range(UMAX):
                     index = lists[side][0, s]
                     halo_out[side][h][0, s] = k_all[h][index]
                     halo_out[side][h][1, s] = v_all[h][index]
-                    if at_once:
-                        halo(side, h, s).start()
-
-    def start_halo(h):
-        for side in range(2):
-            @pl.when(exists[side])
-            def _():
-                for s in range(UMAX):
                     halo(side, h, s).start()
-
-    def each_side(action, h, receive=False):
-        for side in range(2):
-            @pl.when(exists[1 - side if receive else side])
-            def _():
-                action(halo(side, h))
 
     scale = math.log2(math.e) / math.sqrt(HEAD_DIM)
     across = (((1,), (1,)), ((), ()))
@@ -217,6 +216,19 @@
         raised = [jnp.exp2((part - top) * scale) for part in parts]
         total = jnp.sum(functools.reduce(jnp.add, raised), axis=1, keepdims=True)
         return top, total, [one.astype(jnp.bfloat16) for one in raised]
+
+    def picked(side, h, r):
+        key_parts, value_parts, biases = [], [], []
+        for p in range(PICKS):
+            at = 3 * bands + PICKS * 2 * jnp.where(even, side, 1 - side) + p
+            index = meta[r, at]
+            biases.append(jnp.where(meta[r, at + PICKS] > 0, 0.0, MASKED))
+            key_parts.append(halo_in[side][h][0, index])
+            value_parts.append(halo_in[side][h][1, index])
+        far = jnp.concatenate(key_parts, axis=0)
+        scores = lax.dot_general(q_all[h][r], far, across, preferred_element_type=jnp.float32)
+        parts = [scores[:, j * tile : (j + 1) * tile] + bias for j, bias in enumerate(biases)]
+        return parts, jnp.concatenate(value_parts, axis=0)
 
     def attend_near(h, r):
         first = jnp.clip(r - REACH, 0, bands - window)
@@ -226,29 +238,21 @@
             scores[:, j * tile : (j + 1) * tile] + jnp.where(meta[r, bands + first + j] > 0, 0.0, MASKED)
             for j in range(window)
         ]
-        top, total, raised = softmax(parts)
+        more, far = picked(0, h, r)
+        top, total, raised = softmax(parts + more)
         near = v_all[h][pl.ds(first, window)].reshape(window * tile, HEAD_DIM)
-        near_sum[h][r] = jnp.dot(jnp.concatenate(raised, axis=1), near, preferred_element_type=jnp.float32)
+        near_sum[h][r] = jnp.dot(
+            jnp.concatenate(raised[:window], axis=1), near, preferred_element_type=jnp.float32
+        ) + jnp.dot(jnp.concatenate(raised[window:], axis=1), far, preferred_element_type=jnp.float32)
         near_top[h][r] = jnp.broadcast_to(top, (tile, HEAD_DIM))
         near_total[h][r] = jnp.broadcast_to(total, (tile, HEAD_DIM))
 
     def attend_far(h, r):
-        key_parts, value_parts, biases = [], [], []
-        for side in range(2):
-            for p in range(PICKS):
-                at = 3 * bands + 2 * PICKS * (1 - side) + p
-                index = meta[r, at]
-                biases.append(jnp.where(meta[r, at + PICKS] > 0, 0.0, MASKED))
-                key_parts.append(halo_in[side][h][0, index])
-                value_parts.append(halo_in[side][h][1, index])
-        far = jnp.concatenate(key_parts, axis=0)
-        scores = lax.dot_general(q_all[h][r], far, across, preferred_element_type=jnp.float32)
-        parts = [scores[:, j * tile : (j + 1) * tile] + bias for j, bias in enumerate(biases)]
+        parts, far = picked(1, h, r)
         before = near_top[h][r][:, :1]
         top, total, raised = softmax(parts, before)
         kept = jnp.exp2((before - top) * scale)
         total = near_total[h][r][:, :1] * kept + total
-        far = jnp.concatenate(value_parts, axis=0)
         result = jnp.dot(jnp.concatenate(raised, axis=1), far, preferred_element_type=jnp.float32)
         o_all[h][r] = ((near_sum[h][r] * kept + result) / total).astype(o_all[h].dtype)
 
@@ -267,13 +271,16 @@
 
     def near_loop(h):
         wait_spread(2, h)
+        halo(0, h).wait_recv()
 
         @pl.loop(0, bands, unroll=2)
         def _(r):
             attend_near(h, r)
 
     def far_loop(h):
-        each_side(lambda copy: copy.wait_recv(), h, receive=True)
+        @pl.when(exists[1])
+        def _():
+            halo(1, h).wait_recv()
 
         @pl.loop(0, bands // 2)
         def _(i):
@@ -294,15 +301,13 @@
     sent(0, 1)
     sent(1, 1)
     start_spread(2, 0)
+    fill_halo(0)
     start_spread(2, 1)
-    fill_halo(0)
     fill_halo(1)
     near_loop(0)
     near_loop(1)
     far_loop(0)
     far_loop(1)
-    each_side(lambda copy: copy.wait_send(), 0)
-    each_side(lambda copy: copy.wait_send(), 1)
     sent(2, 0)
     sent(2, 1)
 
@@ -310,6 +315,7 @@
         for side in range(2):
             @pl.when(exists[side])
             def _():
+                halo(side, h).wait_send()
                 if h == 0:
                     ask(side).wait_send()
         wait_bytes(o_all[h], o_send.at[h])

time: 153 us -> 152 us (level)
  the two profiles are of different devices: /device:TPU:65 before, /device:TPU:8 now
where the time goes in v5:
time: 152 us
  Pallas kernels  151 us (99%)
    pallas_call x1, Pallas kernels, body(): pl.pallas_call(functools.partial(kernel, bands, groups, heads), out_shape...  151 us

profile of v5, /device:TPU:8, one launch (start us, length us, event | category | flops | bytes accessed | tf_op | source)
XLA Modules:
  0.0 151.5 jit_solution(7024699142319997863)
XLA Ops:
  0.0 150.5 %shard_map.46 = bf16[128,4096]{1,0:T(8,128)(2,1)S(1)} custom-call(s32[16,512]{1,0:T(8,128)} %mask_in.1, bf16[128,4096]{1,0:T(8,128)(2,1)} %q_in.1, bf16[128,4096]{1,0:T(8,128)(2,1)} %k_in.1, bf16[128,4096]{1,0:T(8,128)(2,1)} %v_in.1), custom_call_target="tpu_custom_call" | custom-call | tf_op jit(solution)/shard_map/pallas_call | solution.py:334
  150.5 1.0 copy.6

commit v6 on v5

--- a/solution.py
+++ b/solution.py
@@ -118,14 +118,16 @@
             device_id_type=MESH,
         )
 
-    def start_spread(a, h):
+    def start_spread(arrays, h):
         @pl.loop(0, bands // 2)
         def _(i):
-            spread(a, h, place(i)).start()
+            for a in arrays:
+                spread(a, h, place(i)).start()
 
         @pl.loop(bands // 2 + 1, bands)
         def _(i):
-            spread(a, h, place(i)).start()
+            for a in arrays:
+                spread(a, h, place(i)).start()
 
     def wait_bytes(buffer, sem):
         part = buffer.at[pl.ds(0, bands - 1)]
@@ -138,10 +140,8 @@
     def sent(a, h):
         wait_bytes(moved[a][1][h], send_sem.at[a, h])
 
-    start_spread(0, 0)
-    start_spread(1, 0)
-    start_spread(0, 1)
-    start_spread(1, 1)
+    for h in range(heads):
+        start_spread((0, 1), h)
     for h in range(heads):
         for a in range(3):
             own_copy(a, h).start()
@@ -300,9 +300,9 @@
     sent(1, 0)
     sent(0, 1)
     sent(1, 1)
-    start_spread(2, 0)
+    start_spread((2,), 0)
     fill_halo(0)
-    start_spread(2, 1)
+    start_spread((2,), 1)
     fill_halo(1)
     near_loop(0)
     near_loop(1)

time: 152 us -> 150 us (0.987)
  the two profiles are of different devices: /device:TPU:8 before, /device:TPU:379 now
where the time goes in v6:
time: 150 us
  Pallas kernels  149 us (99%)
    pallas_call x1, Pallas kernels, body(): pl.pallas_call(functools.partial(kernel, bands, groups, heads), out_shape...  149 us

profile of v6, /device:TPU:379, one launch (start us, length us, event | category | flops | bytes accessed | tf_op | source)
XLA Modules:
  0.0 150.2 jit_solution(11404274895907026697)
XLA Ops:
  0.0 149.3 %shard_map.46 = bf16[128,4096]{1,0:T(8,128)(2,1)S(1)} custom-call(s32[16,512]{1,0:T(8,128)} %mask_in.1, bf16[128,4096]{1,0:T(8,128)(2,1)} %q_in.1, bf16[128,4096]{1,0:T(8,128)(2,1)} %k_in.1, bf16[128,4096]{1,0:T(8,128)(2,1)} %v_in.1), custom_call_target="tpu_custom_call" | custom-call | tf_op jit(solution)/shard_map/pallas_call | solution.py:334
  149.3 1.0 copy.6
